TPU v7x, 32 devices: a whole 2x2x4 slice. The times are simulated.
32 devices in a mesh: grp: 2 (over x), gx: 16 (over z, y, core).
Axes of the slice: x: 2, y: 2, z: 4, core: 2. Of those that a mesh axis runs over, the one named last changes fastest.
Arguments:
- field: float32 [32, 1024, 1024], P('grp', 'gx'), parts along dimension 0, may hold values from -150 to 150
- basis_one: float32 [2048, 256], P('grp'), parts along dimension 0, may hold values from -0.1875 to 0.1875
- start: float32 [1024, 256], replicated, may hold values from -6 to 6
Outputs:
- basis_two: float32 [2048, 256], P('grp'), parts along dimension 0
- core: float32 [32, 256, 256], P(('grp', 'gx')), parts along dimension 0
There are 2 independent parts, one for each index of `grp`. A program takes and returns all parts, laid end to end along the dimension named above; an argument that names none is the same for every part. Nothing has to cross between parts.
All inputs are finite; a program needn't handle non-finite values.
Results may differ from a plain program's by a relative error of at most 0.0003.
Values sent between devices are 32-bit elements; how exact they have to be, the bound alone decides.
A program may use at most 128 MiB of HBM per device.

v0:
```python
import jax
import jax.numpy as jnp
from jax import lax
from jax.experimental import pallas as pl
from jax.experimental.pallas import tpu as pltpu
from jax.sharding import PartitionSpec as P

ITERS = 4
BLOCK = 128
SUB = 8
HIGHEST = lax.Precision.HIGHEST


def packed_gram(compressed):
    width = compressed.shape[2]
    rows = [
        jnp.einsum("kri,krj->ij", compressed[:, :, at:at + BLOCK], compressed[:, :, at:], precision=HIGHEST)
        for at in range(0, width, BLOCK)
    ]
    return jnp.concatenate(rows, axis=1)


def unpacked_gram(packed, width):
    rows, offset = [], 0
    for at in range(0, width, BLOCK):
        rows.append(packed[:, offset:offset + width - at])
        offset += width - at
    whole = []
    for a in range(len(rows)):
        below = [rows[b][:, (a - b) * BLOCK:(a - b + 1) * BLOCK].T for b in range(a)]
        whole.append(jnp.concatenate(below + [rows[a]], axis=1))
    return jnp.concatenate(whole, axis=0)


def block_inverse(block):
    size = block.shape[0]
    sub = lax.broadcasted_iota(jnp.int32, (SUB, size), 0)
    lane = lax.broadcasted_iota(jnp.int32, (SUB, size), 1)
    tiles = size // SUB
    left = [block[t * SUB:(t + 1) * SUB, :] for t in range(tiles)]
    right = [jnp.where(lane == sub + t * SUB, 1.0, 0.0).astype(jnp.float32) for t in range(tiles)]
    done = [jnp.zeros((SUB, size), jnp.float32) for t in range(tiles)]

    def row(tile, at):
        return jnp.broadcast_to(tile[at:at + 1, :], (SUB, size))

    def column(tile, at):
        return jnp.broadcast_to(tile[:, at:at + 1], (SUB, size))

    for j in range(0, size, 4):
        tile, at = j // SUB, j % SUB
        m = [row(left[tile], at + k) for k in range(4)]
        n = [row(right[tile], at + k) for k in range(4)]
        cols = [column(left[tile], j + l) for l in range(4)]
        d = [[row(cols[l], at + k) for l in range(k + 1)] for k in range(4)]
        qa = 1.0 / (d[0][0] * d[1][1] - d[1][0] * d[1][0])
        g = {}
        for i in (2, 3):
            g[i, 0] = (d[1][1] * d[i][0] - d[1][0] * d[i][1]) * qa
            g[i, 1] = (d[0][0] * d[i][1] - d[1][0] * d[i][0]) * qa
        e22 = d[2][2] - (g[2, 0] * d[2][0] + g[2, 1] * d[2][1])
        e32 = d[3][2] - (g[3, 0] * d[2][0] + g[3, 1] * d[2][1])
        e33 = d[3][3] - (g[3, 0] * d[3][0] + g[3, 1] * d[3][1])
        qb = 1.0 / (e22 * e33 - e32 * e32)

        def weights(v):
            a0 = (d[1][1] * v[0] - d[1][0] * v[1]) * qa
            a1 = (d[0][0] * v[1] - d[1][0] * v[0]) * qa
            v2 = v[2] - (g[2, 0] * v[0] + g[2, 1] * v[1])
            v3 = v[3] - (g[3, 0] * v[0] + g[3, 1] * v[1])
            b0 = (e33 * v2 - e32 * v3) * qb
            b1 = (e22 * v3 - e32 * v2) * qb
            return (a0 - g[2, 0] * b0 - g[3, 0] * b1, a1 - g[2, 1] * b0 - g[3, 1] * b1, b0, b1), v2, v3

        wm, _, _ = weights(m)
        wn, n2, n3 = weights(n)
        ra = 1.0 / d[0][0]
        rb = 1.0 / e22
        n1 = n[1] - d[1][0] * ra * n[0]
        n3 = n3 - e32 * rb * n2
        p1 = d[1][1] - d[1][0] * d[1][0] * ra
        p3 = e33 - e32 * e32 * rb
        rows = (n[0] * lax.rsqrt(d[0][0]), n1 * lax.rsqrt(p1), n2 * lax.rsqrt(e22), n3 * lax.rsqrt(p3))
        for k in range(4):
            done[tile] = jnp.where(sub == at + k, rows[k], done[tile])
        for t in range(tile, tiles):
            if t == tile and at != 0:
                continue
            c = cols if t == tile else [column(left[t], j + l) for l in range(4)]
            if t == tile:
                c = [jnp.where(sub >= at + 4, v, 0.0) for v in c]
            left[t] = left[t] - ((c[0] * wm[0] + c[1] * wm[1]) + (c[2] * wm[2] + c[3] * wm[3]))
            right[t] = right[t] - ((c[0] * wn[0] + c[1] * wn[1]) + (c[2] * wn[2] + c[3] * wn[3]))
    return jnp.concatenate(done, axis=0)


def dot_t(a, b):
    return lax.dot_general(a, b, (((1,), (1,)), ((), ())), precision=HIGHEST, preferred_element_type=jnp.float32)


def dot(a, b):
    return jnp.dot(a, b, precision=HIGHEST, preferred_element_type=jnp.float32)


def halves_of(value):
    high = value.astype(jnp.bfloat16)
    return high, (value - high.astype(jnp.float32)).astype(jnp.bfloat16)


def dot_halves(a, b):
    def one(x, y):
        return jnp.dot(x, y, preferred_element_type=jnp.float32)

    return one(a[0], b[0]) + (one(a[1], b[0]) + one(a[0], b[1]))


def factor_inverse(cross, inverse_ref, work_ref, part_ref):
    size = cross.shape[0]
    half = size // 2
    eye = lax.broadcasted_iota(jnp.int32, (size, size), 0) == lax.broadcasted_iota(jnp.int32, (size, size), 1)
    diagonal = jnp.where(eye, cross, 0.0)
    along = lax.rsqrt(jnp.sum(diagonal, axis=0, keepdims=True))
    down = lax.rsqrt(jnp.sum(diagonal, axis=1, keepdims=True))
    work_ref[...] = cross * down * along
    part_ref[0] = work_ref[:half, :half]

    def step(index, carry):
        part_ref[index] = block_inverse(part_ref[index])

        @pl.when(index == 0)
        def _():
            side = dot_t(work_ref[half:, :half], part_ref[0])
            work_ref[half:, :half] = side
            part_ref[1] = work_ref[half:, half:] - dot_t(side, side)

        return carry

    lax.fori_loop(0, 2, step, 0)
    first, second = part_ref[0], part_ref[1]
    corner = -dot(dot(second, work_ref[half:, :half]), first)
    inverse_ref[:half, :half] = first * along[:, :half]
    inverse_ref[:half, half:] = jnp.zeros((half, half), jnp.float32)
    inverse_ref[half:, :half] = corner * along[:, :half]
    inverse_ref[half:, half:] = second * along[:, half:]


def subspace_kernel(gram_ref, start_ref, basis_ref, turned_ref, high_ref, low_ref, product_ref, inverse_ref, work_ref,
                    part_ref):
    high_ref[...], low_ref[...] = halves_of(gram_ref[...])
    turned_ref[...] = start_ref[...].T

    def step(index, carry):
        product_ref[...] = dot_halves(halves_of(turned_ref[...]), (high_ref[...], low_ref[...]))
        product = product_ref[...]
        factor_inverse(dot_t(product, product), inverse_ref, work_ref, part_ref)
        turned_ref[...] = dot_halves(halves_of(inverse_ref[...]), halves_of(product_ref[...]))
        return carry

    lax.fori_loop(0, ITERS, step, 0)
    basis_ref[...] = turned_ref[...].T


def subspace(gram, start):
    width, rank = start.shape
    vmem = pl.BlockSpec(memory_space=pltpu.VMEM)
    return pl.pallas_call(
        subspace_kernel,
        out_shape=(jax.ShapeDtypeStruct((width, rank), jnp.float32), jax.ShapeDtypeStruct((rank, width), jnp.float32)),
        in_specs=[vmem, vmem],
        out_specs=(vmem, vmem),
        scratch_shapes=[
            pltpu.VMEM((width, width), jnp.bfloat16),
            pltpu.VMEM((width, width), jnp.bfloat16),
            pltpu.VMEM((rank, width), jnp.float32),
            pltpu.VMEM((rank, rank), jnp.float32),
            pltpu.VMEM((rank, rank), jnp.float32),
            pltpu.VMEM((2, rank // 2, rank // 2), jnp.float32),
        ],
        compiler_params=pltpu.CompilerParams(vmem_limit_bytes=40 * 2**20),
        name="subspace",
    )(gram, start)


HALVES = ((0, 1, 5), (2, 3, 4, 6, 7))


def use_kernel(ranks, width):
    return ranks == 16 and width == 8 * BLOCK


def sum_kernel(part_ref, gram_ref, total, side, near, far, near_sum, far_sum, send_sems, recv_sems):
    me = lax.axis_index("gx")
    c, b, a = lax.rem(me, 2), lax.rem(me // 2, 2), me // 4
    sibling = me + 1 - 2 * c
    across = me + 2 - 4 * b
    others = [lax.rem(a + d, 4) * 4 + b * 2 + c for d in (1, 2, 3)]
    places = [lax.rem(a + d, 4) for d in (1, 2, 3)]

    barrier = pltpu.get_barrier_semaphore()
    for device in [sibling, across] + others:
        pl.semaphore_signal(barrier, inc=1, device_id={"gx": device}, device_id_type=pl.DeviceIdType.MESH)
    pl.semaphore_wait(barrier, 5)

    def send(slot, source, target, device):
        copy = pltpu.make_async_remote_copy(
            src_ref=source, dst_ref=target, send_sem=send_sems.at[slot], recv_sem=recv_sems.at[slot],
            device_id={"gx": device}, device_id_type=pl.DeviceIdType.MESH)
        copy.start()
        return copy

    def rows(start, count):
        return pl.ds(pl.multiple_of(start, SUB), count)

    def finish(copies):
        for copy in copies:
            copy.wait()

    scatter = [send(h, part_ref.at[h, rows((1 - c) * 64, 64)], side.at[h], sibling) for h in (0, 1)]
    scatter[0].wait()
    side[0] = side[0] + part_ref[0, rows(c * 64, 64), :]
    first_near = send(2, side.at[0, rows((1 - b) * 32, 32)], near.at[0, pl.ds(0, 32)], across)
    scatter[1].wait()
    side[1] = side[1] + part_ref[1, rows(c * 64, 64), :]
    first_far = [
        send(3 + d, side.at[1, rows(places[d] * 16, 16)], far.at[1, d, pl.ds(0, 16)], others[d]) for d in range(3)
    ]
    first_near.wait()
    near_sum[...] = side[0, rows(b * 32, 32), :] + near[0]
    second_far = [
        send(6 + d, near_sum.at[rows(places[d] * 8, 8)], far.at[0, d, pl.ds(0, 8)], others[d]) for d in range(3)
    ]
    finish(first_far)
    far_sum[...] = side[1, rows(a * 16, 16), :] + (far[1, 0] + far[1, 1] + far[1, 2])
    second_near = send(9, far_sum.at[rows((1 - b) * 8, 8)], near.at[1, pl.ds(0, 8)], across)
    finish(second_far)
    own_first = c * 64 + b * 32 + a * 8
    total[0, rows(own_first, 8), :] = near_sum[rows(a * 8, 8), :] + (
        far[0, 0, :8, :] + far[0, 1, :8, :] + far[0, 2, :8, :])
    piece = total.at[0, rows(own_first, 8)]
    gather_far = [send(10 + d, piece, piece, others[d]) for d in range(3)]
    second_near.wait()
    own_second = c * 64 + a * 16 + b * 8
    total[1, rows(own_second, 8), :] = far_sum[rows(b * 8, 8), :] + near[1, :8, :]
    piece = total.at[1, rows(own_second, 8)]
    gather_near = send(13, piece, piece, across)
    finish(gather_far)
    piece = total.at[0, rows(c * 64 + b * 32, 32)]
    last_near = send(14, piece, piece, across)
    gather_near.wait()
    piece = total.at[1, rows(c * 64 + a * 16, 16)]
    last_far = [send(15 + d, piece, piece, others[d]) for d in range(3)]
    last_near.wait()
    piece = total.at[0, rows(c * 64, 64)]
    gather = [send(18, piece, piece, sibling)]
    finish(last_far)
    piece = total.at[1, rows(c * 64, 64)]
    gather.append(send(19, piece, piece, sibling))
    for h in (0, 1):
        gather[h].wait()
        offset = 0
        for r in HALVES[h]:
            for s in range(r, 8):
                tile = total[h, :, offset * BLOCK:(offset + 1) * BLOCK]
                gram_ref[r * BLOCK:(r + 1) * BLOCK, s * BLOCK:(s + 1) * BLOCK] = tile
                if s != r:
                    gram_ref[s * BLOCK:(s + 1) * BLOCK, r * BLOCK:(r + 1) * BLOCK] = tile.T
                offset += 1


def summed_gram(compressed):
    width = compressed.shape[2]
    terms = [
        jnp.concatenate(
            [jnp.einsum("kri,krj->ij", compressed[:, :, r * BLOCK:(r + 1) * BLOCK], compressed[:, :, r * BLOCK:],
                        precision=lax.Precision.HIGH) for r in half], axis=1)
        for half in HALVES
    ]
    part = jnp.stack(terms)
    columns = part.shape[2]
    vmem = pl.BlockSpec(memory_space=pltpu.VMEM)
    return pl.pallas_call(
        sum_kernel,
        out_shape=jax.ShapeDtypeStruct((width, width), jnp.float32),
        in_specs=[vmem],
        out_specs=vmem,
        scratch_shapes=[
            pltpu.VMEM((2, BLOCK, columns), jnp.float32),
            pltpu.VMEM((2, 64, columns), jnp.float32),
            pltpu.VMEM((2, 32, columns), jnp.float32),
            pltpu.VMEM((2, 3, 16, columns), jnp.float32),
            pltpu.VMEM((32, columns), jnp.float32),
            pltpu.VMEM((16, columns), jnp.float32),
            pltpu.SemaphoreType.DMA((20,)),
            pltpu.SemaphoreType.DMA((20,)),
        ],
        compiler_params=pltpu.CompilerParams(collective_id=0, has_side_effects=True, vmem_limit_bytes=40 * 2**20),
        name="sum_gram",
    )(part)


def body(field, basis_one, start):
    planes = lax.all_to_all(field, "gx", split_axis=0, concat_axis=1, tiled=True)
    compressed = jnp.einsum("ir,kij->krj", basis_one, planes, precision=lax.Precision.HIGH)
    if use_kernel(lax.axis_size("gx"), compressed.shape[2]):
        gram = summed_gram(compressed)
    else:
        gram = unpacked_gram(lax.psum(packed_gram(compressed), "gx"), compressed.shape[2])
    basis_two, turned = subspace(gram, start)
    core = jnp.einsum("krj,sj->krs", compressed, turned, precision=lax.Precision.HIGH)
    return (basis_two, core)


def solution(mesh):
    in_specs = (P("grp", "gx", None), P("grp", None), P())
    out_specs = (P("grp", None), P(("grp", "gx"), None, None))
    return jax.shard_map(body, mesh=mesh, in_specs=in_specs, out_specs=out_specs, check_vma=False)
```

profile of v0, /device:TPU:0, one launch (start us, length us, event | category | flops | bytes accessed | tf_op | source)
XLA Modules:
  0.0 228.1 jit_solution(5393563876972643576)
XLA Ops:
  0.6 0.0 copy-start
  0.6 99.8 %all_to_all.4 = f32[16,64,1024]{2,1,0:T(8,128)S(1)} all-to-all(f32[16,64,1024]{2,1,0:T(8,128)} %param.3), channel_id=1, replica_groups=mesh['grp'=2,'gx'=16] {'gx'}, dimensions={0} | all-to-all | bytes 8388608 | tf_op jit(solution)/shard_map/all_to_all | solution.py:302
  100.4 0.0 copy-done
  100.4 3.5 %fusion.5 = f32[1024,256]{1,0:T(8,128)S(1)} fusion(f32[1024,1024]{1,0:T(8,128)S(1)} %bitcast.68, f32[1024,256]{1,0:T(8,128)S(1)} %copy-done), kind=kOutput, calls=%fused_computation.27 | convolution fusion | flops 1610612736 | bytes 6291456 | tf_op jit(solution)/shard_map/ir,kij->krj/dot_general | solution.py:303
  103.9 0.3 fusion.4
  104.2 0.6 fusion.3
  104.8 0.7 fusion.1
  105.5 0.6 convolution_dynamic-update-slice_fusion
  106.0 0.5 convolution_dynamic-update-slice_fusion.1
  106.5 0.4 convolution_dynamic-update-slice_fusion.2
  106.9 0.3 convolution_dynamic-update-slice_fusion.3
  107.2 0.2 convolution_dynamic-update-slice_fusion.4
  107.4 0.1 maximum_bitcast_fusion
  107.5 0.2 pad_maximum_fusion.part_ref
  107.7 0.0 copy-start.1
  107.7 48.2 %sum_gram.1.gram_ref = f32[1024,1024]{1,0:T(8,128)S(1)} custom-call(f32[2,128,2304]{2,1,0:T(8,128)S(1)} %pad_maximum_fusion.part_ref), custom_call_target="tpu_custom_call" | custom-call | tf_op jit(solution)/shard_map/sum_gram/pallas_call | solution.py:281
  155.9 0.0 copy-done.1
  155.9 70.5 %subspace.1 = (f32[1024,256]{1,0:T(8,128)}, f32[256,1024]{1,0:T(8,128)S(1)}) custom-call(f32[1024,1024]{1,0:T(8,128)S(1)} %sum_gram.1.gram_ref, f32[1024,256]{1,0:T(8,128)S(1)} %copy-done.1), custom_call_target="tpu_custom_call" | custom-call | tf_op jit(solution)/shard_map/subspace/pallas_call | solution.py:166
  226.4 1.7 convolution_bitcast_fusion
Async XLA Ops:
  0.6 99.8 %copy-start = (f32[1024,256]{1,0:T(8,128)S(1)}, f32[1024,256]{1,0:T(8,128)}, u32[]{:S(2)}) copy-start(f32[1024,256]{1,0:T(8,128)} %param.4) | copy-start | bytes 3145732
  107.7 48.2 %copy-start.1 = (f32[1024,256]{1,0:T(8,128)S(1)}, f32[1024,256]{1,0:T(8,128)}, u32[]{:S(2)}) copy-start(f32[1024,256]{1,0:T(8,128)} %start_ref.1) | copy-start | bytes 3145732
where the time goes:
time: 228 us
  Pallas kernels  119 us (52%)
  blocking collectives  99.8 us (44%)
  matrix products  8.65 us (4%)
    all_to_all x1, blocking collectives, body(): lax.all_to_all(field, 'gx', split_axis=0, concat_axis=1, tiled=True)  99.8 us
    pallas_call x1, Pallas kernels, subspace(): pl.pallas_call(subspace_kernel, out_shape=(jax.ShapeDtypeStruct((width, r...  70.5 us
    pallas_call x1, Pallas kernels, summed_gram(): pl.pallas_call(sum_kernel, out_shape=jax.ShapeDtypeStruct((width, width),...  48.2 us

commit v1 on v0

--- a/solution.py
+++ b/solution.py
@@ -39,7 +39,7 @@
     tiles = size // SUB
     left = [block[t * SUB:(t + 1) * SUB, :] for t in range(tiles)]
     right = [jnp.where(lane == sub + t * SUB, 1.0, 0.0).astype(jnp.float32) for t in range(tiles)]
-    done = [jnp.zeros((SUB, size), jnp.float32) for t in range(tiles)]
+    pairs = range(0, SUB, 2)
 
     def row(tile, at):
         return jnp.broadcast_to(tile[at:at + 1, :], (SUB, size))
@@ -47,51 +47,59 @@
     def column(tile, at):
         return jnp.broadcast_to(tile[:, at:at + 1], (SUB, size))
 
-    for j in range(0, size, 4):
-        tile, at = j // SUB, j % SUB
-        m = [row(left[tile], at + k) for k in range(4)]
-        n = [row(right[tile], at + k) for k in range(4)]
-        cols = [column(left[tile], j + l) for l in range(4)]
-        d = [[row(cols[l], at + k) for l in range(k + 1)] for k in range(4)]
-        qa = 1.0 / (d[0][0] * d[1][1] - d[1][0] * d[1][0])
-        g = {}
-        for i in (2, 3):
-            g[i, 0] = (d[1][1] * d[i][0] - d[1][0] * d[i][1]) * qa
-            g[i, 1] = (d[0][0] * d[i][1] - d[1][0] * d[i][0]) * qa
-        e22 = d[2][2] - (g[2, 0] * d[2][0] + g[2, 1] * d[2][1])
-        e32 = d[3][2] - (g[3, 0] * d[2][0] + g[3, 1] * d[2][1])
-        e33 = d[3][3] - (g[3, 0] * d[3][0] + g[3, 1] * d[3][1])
-        qb = 1.0 / (e22 * e33 - e32 * e32)
-
-        def weights(v):
-            a0 = (d[1][1] * v[0] - d[1][0] * v[1]) * qa
-            a1 = (d[0][0] * v[1] - d[1][0] * v[0]) * qa
-            v2 = v[2] - (g[2, 0] * v[0] + g[2, 1] * v[1])
-            v3 = v[3] - (g[3, 0] * v[0] + g[3, 1] * v[1])
-            b0 = (e33 * v2 - e32 * v3) * qb
-            b1 = (e22 * v3 - e32 * v2) * qb
-            return (a0 - g[2, 0] * b0 - g[3, 0] * b1, a1 - g[2, 1] * b0 - g[3, 1] * b1, b0, b1), v2, v3
-
-        wm, _, _ = weights(m)
-        wn, n2, n3 = weights(n)
-        ra = 1.0 / d[0][0]
-        rb = 1.0 / e22
-        n1 = n[1] - d[1][0] * ra * n[0]
-        n3 = n3 - e32 * rb * n2
-        p1 = d[1][1] - d[1][0] * d[1][0] * ra
-        p3 = e33 - e32 * e32 * rb
-        rows = (n[0] * lax.rsqrt(d[0][0]), n1 * lax.rsqrt(p1), n2 * lax.rsqrt(e22), n3 * lax.rsqrt(p3))
-        for k in range(4):
-            done[tile] = jnp.where(sub == at + k, rows[k], done[tile])
-        for t in range(tile, tiles):
-            if t == tile and at != 0:
-                continue
-            c = cols if t == tile else [column(left[t], j + l) for l in range(4)]
-            if t == tile:
-                c = [jnp.where(sub >= at + 4, v, 0.0) for v in c]
-            left[t] = left[t] - ((c[0] * wm[0] + c[1] * wm[1]) + (c[2] * wm[2] + c[3] * wm[3]))
-            right[t] = right[t] - ((c[0] * wn[0] + c[1] * wn[1]) + (c[2] * wn[2] + c[3] * wn[3]))
-    return jnp.concatenate(done, axis=0)
+    for tile in range(tiles):
+        cols = [column(left[tile], tile * SUB + k) for k in range(SUB)]
+        d = [[row(cols[l], k) for l in range(k + 1)] for k in range(SUB)]
+        g = [[None] * SUB for k in range(SUB)]
+        inverse = {}
+        for a in pairs:
+            b = a + 1
+            inverse[a] = 1.0 / (d[a][a] * d[b][b] - d[b][a] * d[b][a])
+            for i in range(b + 1, SUB):
+                g[i][a] = (d[b][b] * d[i][a] - d[b][a] * d[i][b]) * inverse[a]
+                g[i][b] = (d[a][a] * d[i][b] - d[b][a] * d[i][a]) * inverse[a]
+            for i in range(b + 1, SUB):
+                for l in range(b + 1, i + 1):
+                    d[i][l] = d[i][l] - (g[i][a] * d[l][a] + g[i][b] * d[l][b])
+
+        def forward(v):
+            v = list(v)
+            for a in pairs:
+                for i in range(a + 2, SUB):
+                    v[i] = v[i] - (g[i][a] * v[a] + g[i][a + 1] * v[a + 1])
+            return v
+
+        def backward(v):
+            w = [None] * SUB
+            for a in pairs:
+                b = a + 1
+                w[a] = (d[b][b] * v[a] - d[b][a] * v[b]) * inverse[a]
+                w[b] = (d[a][a] * v[b] - d[b][a] * v[a]) * inverse[a]
+            for a in reversed(pairs):
+                for j in range(a):
+                    w[j] = w[j] - (g[a][j] * w[a] + g[a + 1][j] * w[a + 1])
+            return w
+
+        wm = backward(forward([row(left[tile], k) for k in range(SUB)]))
+        vn = forward([row(right[tile], k) for k in range(SUB)])
+        wn = backward(vn)
+        done = right[tile]
+        for a in pairs:
+            b = a + 1
+            ratio = d[b][a] / d[a][a]
+            done = jnp.where(sub == a, vn[a] * lax.rsqrt(d[a][a]), done)
+            done = jnp.where(sub == b, (vn[b] - ratio * vn[a]) * lax.rsqrt(d[b][b] - ratio * d[b][a]), done)
+        right[tile] = done
+        for t in range(tile + 1, tiles):
+            c = [column(left[t], tile * SUB + k) for k in range(SUB)]
+
+            def total(w):
+                p = [c[k] * w[k] for k in range(SUB)]
+                return ((p[0] + p[1]) + (p[2] + p[3])) + ((p[4] + p[5]) + (p[6] + p[7]))
+
+            left[t] = left[t] - total(wm)
+            right[t] = right[t] - total(wn)
+    return jnp.concatenate(right, axis=0)
 
 
 def dot_t(a, b):
@@ -188,7 +196,7 @@
     return ranks == 16 and width == 8 * BLOCK
 
 
-def sum_kernel(part_ref, gram_ref, total, side, near, far, near_sum, far_sum, send_sems, recv_sems):
+def sum_kernel(plane_ref, gram_ref, part_ref, high_ref, low_ref, turned_high_ref, turned_low_ref, total, side, near, far, near_sum, far_sum, send_sems, recv_sems):
     me = lax.axis_index("gx")
     c, b, a = lax.rem(me, 2), lax.rem(me // 2, 2), me // 4
     sibling = me + 1 - 2 * c
@@ -199,6 +207,21 @@
     barrier = pltpu.get_barrier_semaphore()
     for device in [sibling, across] + others:
         pl.semaphore_signal(barrier, inc=1, device_id={"gx": device}, device_id_type=pl.DeviceIdType.MESH)
+
+    high_ref[...], low_ref[...] = halves_of(plane_ref[...])
+    turned_high_ref[...], turned_low_ref[...] = halves_of(plane_ref[...].T)
+
+    def multiply(h):
+        offset = 0
+        for r in HALVES[h]:
+            at = r * BLOCK
+            wide = plane_ref.shape[1] - at
+            part_ref[h, :, offset:offset + wide] = dot_halves(
+                (turned_high_ref[at:at + BLOCK, :], turned_low_ref[at:at + BLOCK, :]),
+                (high_ref[:, at:], low_ref[:, at:]))
+            offset += wide
+
+    multiply(0)
     pl.semaphore_wait(barrier, 5)
 
     def send(slot, source, target, device):
@@ -215,7 +238,9 @@
         for copy in copies:
             copy.wait()
 
-    scatter = [send(h, part_ref.at[h, rows((1 - c) * 64, 64)], side.at[h], sibling) for h in (0, 1)]
+    scatter = [send(0, part_ref.at[0, rows((1 - c) * 64, 64)], side.at[0], sibling)]
+    multiply(1)
+    scatter.append(send(1, part_ref.at[1, rows((1 - c) * 64, 64)], side.at[1], sibling))
     scatter[0].wait()
     side[0] = side[0] + part_ref[0, rows(c * 64, 64), :]
     first_near = send(2, side.at[0, rows((1 - b) * 32, 32)], near.at[0, pl.ds(0, 32)], across)
@@ -269,14 +294,8 @@
 
 def summed_gram(compressed):
     width = compressed.shape[2]
-    terms = [
-        jnp.concatenate(
-            [jnp.einsum("kri,krj->ij", compressed[:, :, r * BLOCK:(r + 1) * BLOCK], compressed[:, :, r * BLOCK:],
-                        precision=lax.Precision.HIGH) for r in half], axis=1)
-        for half in HALVES
-    ]
-    part = jnp.stack(terms)
-    columns = part.shape[2]
+    rank = compressed.shape[1]
+    columns = sum(8 - r for r in HALVES[0]) * BLOCK
     vmem = pl.BlockSpec(memory_space=pltpu.VMEM)
     return pl.pallas_call(
         sum_kernel,
@@ -284,6 +303,11 @@
         in_specs=[vmem],
         out_specs=vmem,
         scratch_shapes=[
+            pltpu.VMEM((2, BLOCK, columns), jnp.float32),
+            pltpu.VMEM((rank, width), jnp.bfloat16),
+            pltpu.VMEM((rank, width), jnp.bfloat16),
+            pltpu.VMEM((width, rank), jnp.bfloat16),
+            pltpu.VMEM((width, rank), jnp.bfloat16),
             pltpu.VMEM((2, BLOCK, columns), jnp.float32),
             pltpu.VMEM((2, 64, columns), jnp.float32),
             pltpu.VMEM((2, 32, columns), jnp.float32),
@@ -295,15 +319,101 @@
         ],
         compiler_params=pltpu.CompilerParams(collective_id=0, has_side_effects=True, vmem_limit_bytes=40 * 2**20),
         name="sum_gram",
-    )(part)
+    )(compressed[0])
+
+
+def compress_kernel(field_ref, basis_ref, out_ref, first, second, partial, arrived, high_ref, low_ref, send_sems,
+                    recv_sems, local_sems):
+    me = lax.axis_index("gx")
+    half, place = me // 8, lax.rem(me, 8)
+    partner = lax.rem(me + 8, 16)
+    places = [lax.rem(place + d, 8) for d in range(1, 8)]
+    depth = field_ref.shape[1]
+
+    barrier = pltpu.get_barrier_semaphore()
+    for device in [half * 8 + p for p in places] + [partner]:
+        pl.semaphore_signal(barrier, inc=1, device_id={"gx": device}, device_id_type=pl.DeviceIdType.MESH)
+    pl.semaphore_wait(barrier, 8)
+
+    def send(slot, source, target, device):
+        copy = pltpu.make_async_remote_copy(
+            src_ref=source, dst_ref=target, send_sem=send_sems.at[slot], recv_sem=recv_sems.at[slot],
+            device_id={"gx": device}, device_id_type=pl.DeviceIdType.MESH)
+        copy.start()
+        return copy
+
+    def send_first(d):
+        return send(d, field_ref.at[(1 - half) * 8 + places[d]], first.at[place], half * 8 + places[d])
+
+    def send_second(d):
+        return send(7 + d, field_ref.at[half * 8 + places[d]], second.at[place], half * 8 + places[d])
+
+    firsts = [send_first(d) for d in range(7)]
+    own = [
+        pltpu.make_async_copy(field_ref.at[partner], first.at[place], local_sems.at[0]),
+        pltpu.make_async_copy(field_ref.at[me], second.at[place], local_sems.at[1]),
+    ]
+    for copy in own:
+        copy.start()
+    rows = basis_ref[pl.ds(pl.multiple_of(half * (8 * depth), 8), 8 * depth), :]
+    high_ref[...], low_ref[...] = halves_of(rows.T)
+
+    def compress(source, target):
+        width = target.shape[1]
+        for at in range(0, width, 256):
+            block = source[:, :, at:at + 256].reshape(8 * depth, 256)
+            target[:, at:at + 256] = dot_halves((high_ref[...], low_ref[...]), halves_of(block))
+
+    for copy in own:
+        copy.wait()
+    for copy in firsts[:4]:
+        copy.wait()
+    seconds = [send_second(d) for d in range(3)]
+    for copy in firsts[4:]:
+        copy.wait()
+    compress(first, partial)
+    crossing = send(14, partial, arrived, partner)
+    seconds += [send_second(d) for d in range(3, 7)]
+    for copy in seconds:
+        copy.wait()
+    compress(second, out_ref)
+    crossing.wait()
+    out_ref[...] = out_ref[...] + arrived[...]
+
+
+def compressed_plane(field, basis_one):
+    planes, depth, width = field.shape
+    rank = basis_one.shape[1]
+    vmem = pl.BlockSpec(memory_space=pltpu.VMEM)
+    out = pl.pallas_call(
+        compress_kernel,
+        out_shape=jax.ShapeDtypeStruct((rank, width), jnp.float32),
+        in_specs=[pl.BlockSpec(memory_space=pl.ANY), vmem],
+        out_specs=vmem,
+        scratch_shapes=[
+            pltpu.VMEM((8, depth, width), jnp.float32),
+            pltpu.VMEM((8, depth, width), jnp.float32),
+            pltpu.VMEM((rank, width), jnp.float32),
+            pltpu.VMEM((rank, width), jnp.float32),
+            pltpu.VMEM((rank, 8 * depth), jnp.bfloat16),
+            pltpu.VMEM((rank, 8 * depth), jnp.bfloat16),
+            pltpu.SemaphoreType.DMA((15,)),
+            pltpu.SemaphoreType.DMA((15,)),
+            pltpu.SemaphoreType.DMA((2,)),
+        ],
+        compiler_params=pltpu.CompilerParams(collective_id=1, has_side_effects=True, vmem_limit_bytes=40 * 2**20),
+        name="compress",
+    )(field, basis_one)
+    return out[None]
 
 
 def body(field, basis_one, start):
-    planes = lax.all_to_all(field, "gx", split_axis=0, concat_axis=1, tiled=True)
-    compressed = jnp.einsum("ir,kij->krj", basis_one, planes, precision=lax.Precision.HIGH)
-    if use_kernel(lax.axis_size("gx"), compressed.shape[2]):
+    if use_kernel(lax.axis_size("gx"), field.shape[2]) and field.shape[0] == 16:
+        compressed = compressed_plane(field, basis_one)
         gram = summed_gram(compressed)
     else:
+        planes = lax.all_to_all(field, "gx", split_axis=0, concat_axis=1, tiled=True)
+        compressed = jnp.einsum("ir,kij->krj", basis_one, planes, precision=lax.Precision.HIGH)
         gram = unpacked_gram(lax.psum(packed_gram(compressed), "gx"), compressed.shape[2])
     basis_two, turned = subspace(gram, start)
     core = jnp.einsum("krj,sj->krs", compressed, turned, precision=lax.Precision.HIGH)

time: 228 us -> 188 us (0.82)
  blocking collectives: 99.8 us -> 0 us
  Pallas kernels: 119 us -> 182 us
  matrix products: 8.65 us -> 1.32 us
  local copies, waits for them, and re-layouts: 0.02 us -> 3.41 us
    all_to_all x1 -> x0, blocking collectives: 99.8 us -> none  [body(): lax.all_to_all(field, 'gx', split_axis=0, concat_axis=1, tiled=True)]
    pallas_call x0 -> x1, Pallas kernels: none -> 77.8 us  [compressed_plane(): pl.pallas_call(compress_kernel, out_shape=jax.ShapeDtypeStruct((rank, wid...]
    pallas_call x1, Pallas kernels: 70.5 us -> 57.4 us  [subspace(): pl.pallas_call(subspace_kernel, out_shape=(jax.ShapeDtypeStruct((width, r...]
    dot_general x9 -> x0, matrix products: 6.95 us -> none  [the longest x8 3.49 us: summed_gram(): jnp.einsum('kri,krj->ij', compressed[:, :, r * BLOCK:(r + 1) * BLOCK], co...]
    unnamed x4 -> x6, local copies, waits for them, and re-layouts: 0.02 us -> 3.41 us
where the time goes in v1:
time: 188 us
  Pallas kernels  182 us (97%)
  local copies, waits for them, and re-layouts  3.41 us (2%)
    pallas_call x1, Pallas kernels, compressed_plane(): pl.pallas_call(compress_kernel, out_shape=jax.ShapeDtypeStruct((rank, wid...  77.8 us
    pallas_call x1, Pallas kernels, subspace(): pl.pallas_call(subspace_kernel, out_shape=(jax.ShapeDtypeStruct((width, r...  57.4 us
    pallas_call x1, Pallas kernels, summed_gram(): pl.pallas_call(sum_kernel, out_shape=jax.ShapeDtypeStruct((width, width),...  46.9 us

profile of v1, /device:TPU:0, one launch (start us, length us, event | category | flops | bytes accessed | tf_op | source)
XLA Modules:
  0.0 187.6 jit_solution(8629108027327470031)
XLA Ops:
  0.6 0.0 copy-start
  0.6 2.2 %copy-done = f32[16,64,1024]{2,1,0:T(8,128)S(1)} copy-done((f32[16,64,1024]{2,1,0:T(8,128)S(1)}, f32[16,64,1024]{2,1,0:T(8,128)}, u32[]{:S(2)}) %copy-start) | copy-done | bytes 4194328
  2.8 0.0 copy-start.2
  2.8 1.2 copy-done.2
  4.0 0.0 copy-start.1
  4.0 77.8 %compress.1.plane_ref = f32[256,1024]{1,0:T(8,128)S(1)} custom-call(f32[16,64,1024]{2,1,0:T(8,128)S(1)} %copy-done, f32[1024,256]{1,0:T(8,128)S(1)} %copy-done.2), custom_call_target="tpu_custom_call" | custom-call | tf_op jit(solution)/shard_map/compress/pallas_call | solution.py:388
  81.9 46.9 %sum_gram.1.gram_ref = f32[1024,1024]{1,0:T(8,128)S(1)} custom-call(f32[256,1024]{1,0:T(8,128)S(1)} %compress.1.plane_ref), custom_call_target="tpu_custom_call" | custom-call | tf_op jit(solution)/shard_map/sum_gram/pallas_call | solution.py:300
  128.8 0.0 copy-done.1
  128.8 57.4 %subspace.1 = (f32[1024,256]{1,0:T(8,128)}, f32[256,1024]{1,0:T(8,128)S(1)}) custom-call(f32[1024,1024]{1,0:T(8,128)S(1)} %sum_gram.1.gram_ref, f32[1024,256]{1,0:T(8,128)S(1)} %copy-done.1), custom_call_target="tpu_custom_call" | custom-call | tf_op jit(solution)/shard_map/subspace/pallas_call | solution.py:174
  186.2 1.3 convolution_bitcast_fusion
Async XLA Ops:
  0.6 2.2 %copy-start = (f32[16,64,1024]{2,1,0:T(8,128)S(1)}, f32[16,64,1024]{2,1,0:T(8,128)}, u32[]{:S(2)}) copy-start(f32[16,64,1024]{2,1,0:T(8,128)} %field_ref.1) | copy-start | bytes 12582916
  2.8 1.2 copy-start.2
  4.0 124.7 %copy-start.1 = (f32[1024,256]{1,0:T(8,128)S(1)}, f32[1024,256]{1,0:T(8,128)}, u32[]{:S(2)}) copy-start(f32[1024,256]{1,0:T(8,128)} %start_ref.1) | copy-start | bytes 3145732

commit v2 on v1

--- a/solution.py
+++ b/solution.py
@@ -8,6 +8,7 @@
 ITERS = 4
 BLOCK = 128
 SUB = 8
+LIMITS = (140.0, 45.0)
 HIGHEST = lax.Precision.HIGHEST
 
 
@@ -150,6 +151,7 @@
     inverse_ref[:half, half:] = jnp.zeros((half, half), jnp.float32)
     inverse_ref[half:, :half] = corner * along[:, :half]
     inverse_ref[half:, half:] = second * along[:, half:]
+    return jnp.where(eye[:half, :half], jnp.maximum(first, second) + 0.0 * (first + second), 0.0)
 
 
 def subspace_kernel(gram_ref, start_ref, basis_ref, turned_ref, high_ref, low_ref, product_ref, inverse_ref, work_ref,
@@ -157,14 +159,33 @@
     high_ref[...], low_ref[...] = halves_of(gram_ref[...])
     turned_ref[...] = start_ref[...].T
 
+
     def step(index, carry):
+        full, poor = carry
         product_ref[...] = dot_halves(halves_of(turned_ref[...]), (high_ref[...], low_ref[...]))
         product = product_ref[...]
-        factor_inverse(dot_t(product, product), inverse_ref, work_ref, part_ref)
-        turned_ref[...] = dot_halves(halves_of(inverse_ref[...]), halves_of(product_ref[...]))
-        return carry
-
-    lax.fori_loop(0, ITERS, step, 0)
+        limit = jnp.where(index == ITERS - 1, LIMITS[1], LIMITS[0])
+
+        def factored():
+            roots = factor_inverse(dot_t(product, product), inverse_ref, work_ref, part_ref)
+            turned_ref[...] = dot_halves(halves_of(inverse_ref[...]), halves_of(product_ref[...]))
+            return jnp.max(jnp.where(roots < limit, 0.0, 1.0))
+
+        def scaled():
+            turned_ref[...] = product * lax.rsqrt(jnp.sum(product * product, axis=1, keepdims=True))
+            return 0.0
+
+        last_of_pair = lax.rem(ITERS - 1 - index, 2) == 0
+        return full, jnp.maximum(poor, lax.cond(full | last_of_pair, factored, scaled))
+
+    def attempt(carry):
+        count, _ = carry
+        turned_ref[...] = start_ref[...].T
+        _, poor = lax.fori_loop(0, ITERS, step, (count > 0, jnp.float32(0.0)))
+        return count + 1, poor
+
+    lax.while_loop(lambda carry: (carry[0] == 0) | ((carry[0] == 1) & (carry[1] > 0.0)), attempt,
+                   (jnp.int32(0), jnp.float32(0.0)))
     basis_ref[...] = turned_ref[...].T
 
 

time: 188 us -> 215 us (1.14)
  Pallas kernels: 182 us -> 209 us
    pallas_call x1, Pallas kernels: 57.4 us -> 84.2 us  [subspace(): pl.pallas_call(subspace_kernel, out_shape=(jax.ShapeDtypeStruct((width, r...]
where the time goes in v2:
time: 215 us; the launch traced here: 214 us
  Pallas kernels  209 us (97%)
  local copies, waits for them, and re-layouts  3.41 us (2%)
    pallas_call x1, Pallas kernels, subspace(): pl.pallas_call(subspace_kernel, out_shape=(jax.ShapeDtypeStruct((width, r...  84.2 us
    pallas_call x1, Pallas kernels, compressed_plane(): pl.pallas_call(compress_kernel, out_shape=jax.ShapeDtypeStruct((rank, wid...  77.8 us
    pallas_call x1, Pallas kernels, summed_gram(): pl.pallas_call(sum_kernel, out_shape=jax.ShapeDtypeStruct((width, width),...  46.9 us

profile of v2, /device:TPU:0, one launch (start us, length us, event | category | flops | bytes accessed | tf_op | source)
XLA Modules:
  0.0 214.4 jit_solution(15962291177556652580)
XLA Ops:
  0.6 0.0 copy-start
  0.6 2.2 %copy-done = f32[16,64,1024]{2,1,0:T(8,128)S(1)} copy-done((f32[16,64,1024]{2,1,0:T(8,128)S(1)}, f32[16,64,1024]{2,1,0:T(8,128)}, u32[]{:S(2)}) %copy-start) | copy-done | bytes 4194328
  2.8 0.0 copy-start.2
  2.8 1.2 copy-done.2
  4.0 0.0 copy-start.1
  4.0 77.8 %compress.1.plane_ref = f32[256,1024]{1,0:T(8,128)S(1)} custom-call(f32[16,64,1024]{2,1,0:T(8,128)S(1)} %copy-done, f32[1024,256]{1,0:T(8,128)S(1)} %copy-done.2), custom_call_target="tpu_custom_call" | custom-call | tf_op jit(solution)/shard_map/compress/pallas_call | solution.py:409
  81.9 46.9 %sum_gram.1.gram_ref = f32[1024,1024]{1,0:T(8,128)S(1)} custom-call(f32[256,1024]{1,0:T(8,128)S(1)} %compress.1.plane_ref), custom_call_target="tpu_custom_call" | custom-call | tf_op jit(solution)/shard_map/sum_gram/pallas_call | solution.py:321
  128.8 0.0 copy-done.1
  128.8 84.2 %subspace.1 = (f32[1024,256]{1,0:T(8,128)}, f32[256,1024]{1,0:T(8,128)S(1)}) custom-call(f32[1024,1024]{1,0:T(8,128)S(1)} %sum_gram.1.gram_ref, f32[1024,256]{1,0:T(8,128)S(1)} %copy-done.1), custom_call_target="tpu_custom_call" | custom-call | tf_op jit(solution)/shard_map/subspace/pallas_call | solution.py:195
  213.0 1.3 convolution_bitcast_fusion
Async XLA Ops:
  0.6 2.2 %copy-start = (f32[16,64,1024]{2,1,0:T(8,128)S(1)}, f32[16,64,1024]{2,1,0:T(8,128)}, u32[]{:S(2)}) copy-start(f32[16,64,1024]{2,1,0:T(8,128)} %field_ref.1) | copy-start | bytes 12582916
  2.8 1.2 copy-start.2
  4.0 124.7 %copy-start.1 = (f32[1024,256]{1,0:T(8,128)S(1)}, f32[1024,256]{1,0:T(8,128)}, u32[]{:S(2)}) copy-start(f32[1024,256]{1,0:T(8,128)} %start_ref.1) | copy-start | bytes 3145732

commit v3 on v2

--- a/solution.py
+++ b/solution.py
@@ -154,15 +154,13 @@
     return jnp.where(eye[:half, :half], jnp.maximum(first, second) + 0.0 * (first + second), 0.0)
 
 
-def subspace_kernel(gram_ref, start_ref, basis_ref, turned_ref, high_ref, low_ref, product_ref, inverse_ref, work_ref,
-                    part_ref):
-    high_ref[...], low_ref[...] = halves_of(gram_ref[...])
+def subspace_kernel(gram_ref, start_ref, basis_ref, turned_ref, product_ref, inverse_ref, work_ref, part_ref):
     turned_ref[...] = start_ref[...].T
 
 
     def step(index, carry):
         full, poor = carry
-        product_ref[...] = dot_halves(halves_of(turned_ref[...]), (high_ref[...], low_ref[...]))
+        product_ref[...] = dot(turned_ref[...], gram_ref[...])
         product = product_ref[...]
         limit = jnp.where(index == ITERS - 1, LIMITS[1], LIMITS[0])
 
@@ -198,8 +196,6 @@
         in_specs=[vmem, vmem],
         out_specs=(vmem, vmem),
         scratch_shapes=[
-            pltpu.VMEM((width, width), jnp.bfloat16),
-            pltpu.VMEM((width, width), jnp.bfloat16),
             pltpu.VMEM((rank, width), jnp.float32),
             pltpu.VMEM((rank, rank), jnp.float32),
             pltpu.VMEM((rank, rank), jnp.float32),
@@ -210,20 +206,21 @@
     )(gram, start)
 
 
-HALVES = ((0, 1, 5), (2, 3, 4, 6, 7))
+CHUNKS = ((0, 7), (1, 6), (2, 5), (3, 4))
 
 
 def use_kernel(ranks, width):
     return ranks == 16 and width == 8 * BLOCK
 
 
-def sum_kernel(plane_ref, gram_ref, part_ref, high_ref, low_ref, turned_high_ref, turned_low_ref, total, side, near, far, near_sum, far_sum, send_sems, recv_sems):
+def sum_kernel(plane_ref, gram_ref, part_ref, high_ref, low_ref, turned_high_ref, turned_low_ref, total, side, near,
+               far, near_sum, send_sems, recv_sems):
     me = lax.axis_index("gx")
     c, b, a = lax.rem(me, 2), lax.rem(me // 2, 2), me // 4
     sibling = me + 1 - 2 * c
     across = me + 2 - 4 * b
-    others = [lax.rem(a + d, 4) * 4 + b * 2 + c for d in (1, 2, 3)]
     places = [lax.rem(a + d, 4) for d in (1, 2, 3)]
+    others = [place * 4 + b * 2 + c for place in places]
 
     barrier = pltpu.get_barrier_semaphore()
     for device in [sibling, across] + others:
@@ -231,19 +228,6 @@
 
     high_ref[...], low_ref[...] = halves_of(plane_ref[...])
     turned_high_ref[...], turned_low_ref[...] = halves_of(plane_ref[...].T)
-
-    def multiply(h):
-        offset = 0
-        for r in HALVES[h]:
-            at = r * BLOCK
-            wide = plane_ref.shape[1] - at
-            part_ref[h, :, offset:offset + wide] = dot_halves(
-                (turned_high_ref[at:at + BLOCK, :], turned_low_ref[at:at + BLOCK, :]),
-                (high_ref[:, at:], low_ref[:, at:]))
-            offset += wide
-
-    multiply(0)
-    pl.semaphore_wait(barrier, 5)
 
     def send(slot, source, target, device):
         copy = pltpu.make_async_remote_copy(
@@ -255,68 +239,79 @@
     def rows(start, count):
         return pl.ds(pl.multiple_of(start, SUB), count)
 
-    def finish(copies):
-        for copy in copies:
+    def spread(q, slot, start, count, devices):
+        piece = total.at[q, rows(start, count)]
+        flying[q] = [send(q * 10 + slot + d, piece, piece, devices[d]) for d in range(len(devices))]
+
+    def arrive(q):
+        for copy in flying[q]:
             copy.wait()
 
-    scatter = [send(0, part_ref.at[0, rows((1 - c) * 64, 64)], side.at[0], sibling)]
-    multiply(1)
-    scatter.append(send(1, part_ref.at[1, rows((1 - c) * 64, 64)], side.at[1], sibling))
-    scatter[0].wait()
-    side[0] = side[0] + part_ref[0, rows(c * 64, 64), :]
-    first_near = send(2, side.at[0, rows((1 - b) * 32, 32)], near.at[0, pl.ds(0, 32)], across)
-    scatter[1].wait()
-    side[1] = side[1] + part_ref[1, rows(c * 64, 64), :]
-    first_far = [
-        send(3 + d, side.at[1, rows(places[d] * 16, 16)], far.at[1, d, pl.ds(0, 16)], others[d]) for d in range(3)
-    ]
-    first_near.wait()
-    near_sum[...] = side[0, rows(b * 32, 32), :] + near[0]
-    second_far = [
-        send(6 + d, near_sum.at[rows(places[d] * 8, 8)], far.at[0, d, pl.ds(0, 8)], others[d]) for d in range(3)
-    ]
-    finish(first_far)
-    far_sum[...] = side[1, rows(a * 16, 16), :] + (far[1, 0] + far[1, 1] + far[1, 2])
-    second_near = send(9, far_sum.at[rows((1 - b) * 8, 8)], near.at[1, pl.ds(0, 8)], across)
-    finish(second_far)
-    own_first = c * 64 + b * 32 + a * 8
-    total[0, rows(own_first, 8), :] = near_sum[rows(a * 8, 8), :] + (
-        far[0, 0, :8, :] + far[0, 1, :8, :] + far[0, 2, :8, :])
-    piece = total.at[0, rows(own_first, 8)]
-    gather_far = [send(10 + d, piece, piece, others[d]) for d in range(3)]
-    second_near.wait()
-    own_second = c * 64 + a * 16 + b * 8
-    total[1, rows(own_second, 8), :] = far_sum[rows(b * 8, 8), :] + near[1, :8, :]
-    piece = total.at[1, rows(own_second, 8)]
-    gather_near = send(13, piece, piece, across)
-    finish(gather_far)
-    piece = total.at[0, rows(c * 64 + b * 32, 32)]
-    last_near = send(14, piece, piece, across)
-    gather_near.wait()
-    piece = total.at[1, rows(c * 64 + a * 16, 16)]
-    last_far = [send(15 + d, piece, piece, others[d]) for d in range(3)]
-    last_near.wait()
-    piece = total.at[0, rows(c * 64, 64)]
-    gather = [send(18, piece, piece, sibling)]
-    finish(last_far)
-    piece = total.at[1, rows(c * 64, 64)]
-    gather.append(send(19, piece, piece, sibling))
-    for h in (0, 1):
-        gather[h].wait()
+    def multiply(q):
         offset = 0
-        for r in HALVES[h]:
+        for r in CHUNKS[q]:
+            at = r * BLOCK
+            wide = plane_ref.shape[1] - at
+            part_ref[q, :, offset:offset + wide] = dot_halves(
+                (turned_high_ref[at:at + BLOCK, :], turned_low_ref[at:at + BLOCK, :]),
+                (high_ref[:, at:], low_ref[:, at:]))
+            offset += wide
+
+    def begin(q):
+        multiply(q)
+        if q == 0:
+            pl.semaphore_wait(barrier, 5)
+        flying[q] = [send(q * 10, part_ref.at[q, rows((1 - c) * 64, 64)], side.at[q], sibling)]
+
+    def scatter_near(q):
+        arrive(q)
+        side[q] = side[q] + part_ref[q, rows(c * 64, 64), :]
+        flying[q] = [send(q * 10 + 1, side.at[q, rows((1 - b) * 32, 32)], near.at[q], across)]
+
+    def scatter_far(q):
+        arrive(q)
+        near_sum[q] = side[q, rows(b * 32, 32), :] + near[q]
+        flying[q] = [
+            send(q * 10 + 2 + d, near_sum.at[q, rows(places[d] * 8, 8)], far.at[q, d], others[d]) for d in range(3)
+        ]
+
+    def gather_far(q):
+        arrive(q)
+        start = c * 64 + b * 32 + a * 8
+        total[q, rows(start, 8), :] = near_sum[q, rows(a * 8, 8), :] + (far[q, 0] + far[q, 1] + far[q, 2])
+        spread(q, 5, start, 8, others)
+
+    def gather_near(q):
+        arrive(q)
+        spread(q, 8, c * 64 + b * 32, 32, [across])
+
+    def gather_side(q):
+        arrive(q)
+        spread(q, 9, c * 64, 64, [sibling])
+
+    def unpack(q):
+        arrive(q)
+        offset = 0
+        for r in CHUNKS[q]:
             for s in range(r, 8):
-                tile = total[h, :, offset * BLOCK:(offset + 1) * BLOCK]
+                tile = total[q, :, offset * BLOCK:(offset + 1) * BLOCK]
                 gram_ref[r * BLOCK:(r + 1) * BLOCK, s * BLOCK:(s + 1) * BLOCK] = tile
                 if s != r:
                     gram_ref[s * BLOCK:(s + 1) * BLOCK, r * BLOCK:(r + 1) * BLOCK] = tile.T
                 offset += 1
 
+    flying = {}
+    stages = (begin, scatter_near, scatter_far, gather_far, gather_near, gather_side, unpack)
+    for tick in range(len(CHUNKS) + len(stages) - 1):
+        for at, stage in enumerate(stages):
+            if 0 <= tick - at < len(CHUNKS):
+                stage(tick - at)
+
 
 def summed_gram(compressed):
     width = compressed.shape[2]
     rank = compressed.shape[1]
-    columns = sum(8 - r for r in HALVES[0]) * BLOCK
+    columns = sum(8 - r for r in CHUNKS[0]) * BLOCK
     vmem = pl.BlockSpec(memory_space=pltpu.VMEM)
     return pl.pallas_call(
         sum_kernel,
@@ -324,19 +319,18 @@
         in_specs=[vmem],
         out_specs=vmem,
         scratch_shapes=[
-            pltpu.VMEM((2, BLOCK, columns), jnp.float32),
+            pltpu.VMEM((4, BLOCK, columns), jnp.float32),
             pltpu.VMEM((rank, width), jnp.bfloat16),
             pltpu.VMEM((rank, width), jnp.bfloat16),
             pltpu.VMEM((width, rank), jnp.bfloat16),
             pltpu.VMEM((width, rank), jnp.bfloat16),
-            pltpu.VMEM((2, BLOCK, columns), jnp.float32),
-            pltpu.VMEM((2, 64, columns), jnp.float32),
-            pltpu.VMEM((2, 32, columns), jnp.float32),
-            pltpu.VMEM((2, 3, 16, columns), jnp.float32),
-            pltpu.VMEM((32, columns), jnp.float32),
-            pltpu.VMEM((16, columns), jnp.float32),
-            pltpu.SemaphoreType.DMA((20,)),
-            pltpu.SemaphoreType.DMA((20,)),
+            pltpu.VMEM((4, BLOCK, columns), jnp.float32),
+            pltpu.VMEM((4, 64, columns), jnp.float32),
+            pltpu.VMEM((4, 32, columns), jnp.float32),
+            pltpu.VMEM((4, 3, 8, columns), jnp.float32),
+            pltpu.VMEM((4, 32, columns), jnp.float32),
+            pltpu.SemaphoreType.DMA((40,)),
+            pltpu.SemaphoreType.DMA((40,)),
         ],
         compiler_params=pltpu.CompilerParams(collective_id=0, has_side_effects=True, vmem_limit_bytes=40 * 2**20),
         name="sum_gram",

time: 215 us -> 223 us (1.037)
  Pallas kernels: 209 us -> 217 us
    pallas_call x1, Pallas kernels: 84.2 us -> 97.3 us  [subspace(): pl.pallas_call(subspace_kernel, out_shape=(jax.ShapeDtypeStruct((width, r...]
    pallas_call x1, Pallas kernels: 46.9 us -> 41.9 us  [summed_gram(): pl.pallas_call(sum_kernel, out_shape=jax.ShapeDtypeStruct((width, width),...]
where the time goes in v3:
time: 223 us; the launch traced here: 222 us
  Pallas kernels  217 us (97%)
  local copies, waits for them, and re-layouts  3.41 us (2%)
    pallas_call x1, Pallas kernels, subspace(): pl.pallas_call(subspace_kernel, out_shape=(jax.ShapeDtypeStruct((width, r...  97.3 us
    pallas_call x1, Pallas kernels, compressed_plane(): pl.pallas_call(compress_kernel, out_shape=jax.ShapeDtypeStruct((rank, wid...  77.8 us
    pallas_call x1, Pallas kernels, summed_gram(): pl.pallas_call(sum_kernel, out_shape=jax.ShapeDtypeStruct((width, width),...  41.9 us

profile of v3, /device:TPU:0, one launch (start us, length us, event | category | flops | bytes accessed | tf_op | source)
XLA Modules:
  0.0 222.4 jit_solution(12915251639171073049)
XLA Ops:
  0.6 0.0 copy-start
  0.6 2.2 copy-done
  2.8 0.0 copy-start.2
  2.8 1.2 copy-done.2
  4.0 0.0 copy-start.1
  4.0 77.8 %compress.1.plane_ref = f32[256,1024]{1,0:T(8,128)S(1)} custom-call(f32[16,64,1024]{2,1,0:T(8,128)S(1)} %copy-done, f32[1024,256]{1,0:T(8,128)S(1)} %copy-done.2), custom_call_target="tpu_custom_call" | custom-call | tf_op jit(solution)/shard_map/compress/pallas_call | solution.py:403
  81.9 41.9 %sum_gram.1.gram_ref = f32[1024,1024]{1,0:T(8,128)S(1)} custom-call(f32[256,1024]{1,0:T(8,128)S(1)} %compress.1.plane_ref), custom_call_target="tpu_custom_call" | custom-call | tf_op jit(solution)/shard_map/sum_gram/pallas_call | solution.py:316
  123.8 0.0 copy-done.1
  123.8 97.3 %subspace.1 = (f32[1024,256]{1,0:T(8,128)}, f32[256,1024]{1,0:T(8,128)S(1)}) custom-call(f32[1024,1024]{1,0:T(8,128)S(1)} %sum_gram.1.gram_ref, f32[1024,256]{1,0:T(8,128)S(1)} %copy-done.1), custom_call_target="tpu_custom_call" | custom-call | tf_op jit(solution)/shard_map/subspace/pallas_call | solution.py:193
  221.1 1.3 convolution_bitcast_fusion
Async XLA Ops:
  0.6 2.2 copy-start
  2.8 1.2 copy-start.2
  4.0 119.7 %copy-start.1 = (f32[1024,256]{1,0:T(8,128)S(1)}, f32[1024,256]{1,0:T(8,128)}, u32[]{:S(2)}) copy-start(f32[1024,256]{1,0:T(8,128)} %start_ref.1) | copy-start | bytes 3145732
